TPU v7x, 32 devices: a whole 2x2x4 slice. The times are simulated.
32 devices in a mesh: img: 8 (over z, x), txt: 4 (over y, core).
Axes of the slice: x: 2, y: 2, z: 4, core: 2. Of those that a mesh axis runs over, the one named last changes fastest.
Arguments:
- image_tokens: bfloat16 [16, 1024, 1024], P('img', 'txt'), may hold values from -6 to 6
- text_states: bfloat16 [8, 128, 1024], P('img', 'txt'), may hold values from -6 to 6
- text_segments: int32 [8, 128], P('img', 'txt'), may hold values from 0 to 1, never falling along the last dimension, each value on 1 to 80 neighbouring positions
- item_segments: int32 [8, 2], P('img'), may hold values from 0 to 1, each once within a row
- norm1_gain: float32 [1024], replicated, may hold values from 0.25 to 1.75
- norm1_bias: float32 [1024], replicated, may hold values from -1.2 to 1.2
- w_qkv: bfloat16 [1024, 3072], replicated, may hold values from -0.1875 to 0.1875
- w_self_out: bfloat16 [1024, 1024], replicated, may hold values from -1.5 to 1.5
- norm2_gain: float32 [1024], replicated, may hold values from 0.25 to 1.75
- norm2_bias: float32 [1024], replicated, may hold values from -1.2 to 1.2
- w_cross_q: bfloat16 [1024, 1024], replicated, may hold values from -0.1875 to 0.1875
- w_cross_kv: bfloat16 [1024, 2048], replicated, may hold values from -0.1875 to 0.1875
- w_cross_out: bfloat16 [1024, 1024], replicated, may hold values from -0.5 to 0.5
- norm3_gain: float32 [1024], replicated, may hold values from 0.25 to 1.75
- norm3_bias: float32 [1024], replicated, may hold values from -1.2 to 1.2
- w_up: bfloat16 [1024, 4096], replicated, may hold values from -0.1875 to 0.1875
- w_down: bfloat16 [4096, 1024], replicated, may hold values from -0.09375 to 0.09375
- cotangent: bfloat16 [16, 1024, 1024], P('img', 'txt'), may hold values from -6 to 6
Outputs:
- block_out: bfloat16 [16, 1024, 1024], P('img', 'txt')
- image_grad: float32 [16, 1024, 1024], P('img', 'txt')
- text_grad: float32 [8, 128, 1024], P('img', 'txt')
- norm1_gain_grad: float32 [1024], P(('img', 'txt'))
- norm1_bias_grad: float32 [1024], P(('img', 'txt'))
- w_qkv_grad: float32 [1024, 3072], P(('img', 'txt'))
- w_self_out_grad: float32 [1024, 1024], P(('img', 'txt'))
- norm2_gain_grad: float32 [1024], P(('img', 'txt'))
- norm2_bias_grad: float32 [1024], P(('img', 'txt'))
- w_cross_q_grad: float32 [1024, 1024], P(('img', 'txt'))
- w_cross_kv_grad: float32 [1024, 2048], P(('img', 'txt'))
- w_cross_out_grad: float32 [1024, 1024], P(('img', 'txt'))
- norm3_gain_grad: float32 [1024], P(('img', 'txt'))
- norm3_bias_grad: float32 [1024], P(('img', 'txt'))
- w_up_grad: float32 [1024, 4096], P(('img', 'txt'))
- w_down_grad: float32 [4096, 1024], P(('img', 'txt'))
Inputs may be any that keep to these rules, and one draw needn't show every extreme that they name: `text_segments`: segment numbers never fall along an encoder row, and every number below 2 occurs in each row. `item_segments`: the items of one index of img name each caption of their encoder row exactly once.
All inputs are finite; a program needn't handle non-finite values.
Results may differ from a plain program's by a relative error of at most 0.018.
Values may be sent and summed in bfloat16 or wider, within the bound.
No kernel may reach another device: no remote copies, remote signals or barrier semaphores. Data moves between devices by JAX's collectives and lax.ppermute only.
A program may use at most 320 MiB of HBM per device.

v0:
```python
from functools import partial

import jax
import jax.numpy as jnp
from jax import lax
from jax.sharding import PartitionSpec as P

D = 1024
HEADS = 16
HEAD = 64
ITEM_LEN = 1024
TEXT_LEN = 128


EPS = 1e-05
MASKED = -1e30


def layer_norm(values, norm_gain, norm_bias):
    center = values - jnp.mean(values, axis=-1, keepdims=True)
    spread = jnp.mean(center * center, axis=-1, keepdims=True)
    return center * lax.rsqrt(spread + EPS) * norm_gain + norm_bias


def project(values, weight):
    return jnp.einsum("...d,de->...e", values, weight, preferred_element_type=jnp.float32)


def back_project(grads, weight):
    return jnp.einsum("...e,de->...d", grads, weight, preferred_element_type=jnp.float32)


def weight_grad(values, grads):
    flat_in = values.reshape(-1, values.shape[-1])
    flat_out = grads.reshape(-1, grads.shape[-1])
    return jnp.einsum("nd,ne->de", flat_in, flat_out, preferred_element_type=jnp.float32)


def softmax_rows(scores):
    top_score = jnp.max(scores, axis=-1, keepdims=True)
    shifted = jnp.exp(scores - top_score)
    total = jnp.sum(shifted, axis=-1, keepdims=True)
    return (shifted / total, top_score + jnp.log(total))


def softmax_back(weights_f, grads):
    return weights_f * (grads - jnp.sum(weights_f * grads, axis=-1, keepdims=True))


def per_device(
    image_tokens,
    text_states,
    text_segments,
    item_segments,
    norm1_gain,
    norm1_bias,
    w_qkv,
    w_self_out,
    norm2_gain,
    norm2_bias,
    w_cross_q,
    w_cross_kv,
    w_cross_out,
    norm3_gain,
    norm3_bias,
    w_up,
    w_down,
    cotangent,
):
    batch_items = image_tokens.shape[0]
    local_len = image_tokens.shape[1]
    score_scale = HEAD ** (-0.5)
    offset = lax.axis_index("txt") * local_len
    tokens = image_tokens.astype(jnp.float32)
    normed1_f, norm1_back = jax.vjp(layer_norm, tokens, norm1_gain, norm1_bias)
    normed1 = normed1_f.astype(jnp.bfloat16)
    joined_qkv = project(normed1, w_qkv).astype(jnp.bfloat16)
    queries = joined_qkv[..., :D].reshape(batch_items, local_len, HEADS, HEAD)
    self_kv = lax.all_gather(joined_qkv[..., D:], "txt", axis=1, tiled=True)
    key_rows = self_kv[..., :D].reshape(batch_items, ITEM_LEN, HEADS, HEAD)
    value_rows = self_kv[..., D:].reshape(batch_items, ITEM_LEN, HEADS, HEAD)
    causal = jnp.arange(ITEM_LEN)[None, :] <= (offset + jnp.arange(local_len))[:, None]

    def self_scores():
        raw_scores = (
            jnp.einsum("ilhe,imhe->ihlm", queries, key_rows, preferred_element_type=jnp.float32)
            * score_scale
        )
        return jnp.where(causal, raw_scores, MASKED)

    attention, self_lse = softmax_rows(self_scores())
    attended = jnp.einsum(
        "ihlm,imhe->ilhe",
        attention.astype(jnp.bfloat16),
        value_rows,
        preferred_element_type=jnp.float32,
    )
    attended = attended.reshape(batch_items, local_len, D).astype(jnp.bfloat16)
    hidden1 = tokens + project(attended, w_self_out)
    normed2_f, norm2_back = jax.vjp(layer_norm, hidden1, norm2_gain, norm2_bias)
    normed2 = normed2_f.astype(jnp.bfloat16)
    cross_queries = (
        project(normed2, w_cross_q)
        .astype(jnp.bfloat16)
        .reshape(batch_items, local_len, HEADS, HEAD)
    )
    id_wire = text_segments.astype(jnp.bfloat16)
    owned_kv = project(text_states, w_cross_kv).astype(jnp.bfloat16)
    text_kv, state_ids = (
        lax.all_gather(owned_kv, "txt", axis=1, tiled=True),
        lax.all_gather(id_wire, "txt", axis=1, tiled=True),
    )
    text_keys = text_kv[0, :, :D].reshape(TEXT_LEN, HEADS, HEAD)
    text_values = text_kv[0, :, D:].reshape(TEXT_LEN, HEADS, HEAD)
    matches = state_ids[0][None, :] == item_segments[0].astype(jnp.bfloat16)[:, None]
    raw_cross = (
        jnp.einsum("ilhe,she->ihls", cross_queries, text_keys, preferred_element_type=jnp.float32)
        * score_scale
    )
    cross_weights, cross_lse = softmax_rows(jnp.where(matches[:, None, None, :], raw_cross, MASKED))
    cross_low = cross_weights.astype(jnp.bfloat16)
    cross_mixed = jnp.einsum(
        "ihls,she->ilhe", cross_low, text_values, preferred_element_type=jnp.float32
    )
    cross_mixed = cross_mixed.reshape(batch_items, local_len, D).astype(jnp.bfloat16)
    hidden2 = hidden1 + project(cross_mixed, w_cross_out)
    normed3_f, norm3_back = jax.vjp(layer_norm, hidden2, norm3_gain, norm3_bias)
    normed3 = normed3_f.astype(jnp.bfloat16)
    up_value = project(normed3, w_up)
    activated_f, gelu_back = jax.vjp(partial(jax.nn.gelu, approximate=False), up_value)
    activated = activated_f.astype(jnp.bfloat16)
    block_out = (hidden2 + project(activated, w_down)).astype(jnp.bfloat16)
    down_grad = weight_grad(activated, cotangent)
    grad_up = gelu_back(back_project(cotangent, w_down))[0].astype(jnp.bfloat16)
    up_grad = weight_grad(normed3, grad_up)
    grad_hidden2, norm3_gain_grad, norm3_bias_grad = norm3_back(back_project(grad_up, w_up))
    grad_hidden2 = grad_hidden2 + cotangent.astype(jnp.float32)
    branch2 = grad_hidden2.astype(jnp.bfloat16)
    cross_out_grad = weight_grad(cross_mixed, branch2)
    grad_cross_mixed = (
        back_project(branch2, w_cross_out)
        .astype(jnp.bfloat16)
        .reshape(batch_items, local_len, HEADS, HEAD)
    )
    grad_cross_weights = jnp.einsum(
        "ilhe,she->ihls", grad_cross_mixed, text_values, preferred_element_type=jnp.float32
    )
    grad_text_values = jnp.einsum(
        "ihls,ilhe->she", cross_low, grad_cross_mixed, preferred_element_type=jnp.float32
    )
    cross_score_grad = softmax_back(cross_weights, grad_cross_weights).astype(jnp.bfloat16)
    grad_cross_queries = (
        jnp.einsum(
            "ihls,she->ilhe", cross_score_grad, text_keys, preferred_element_type=jnp.float32
        )
        * score_scale
    )
    grad_cross_queries = grad_cross_queries.astype(jnp.bfloat16).reshape(batch_items, local_len, D)
    grad_text_keys = (
        jnp.einsum(
            "ihls,ilhe->she", cross_score_grad, cross_queries, preferred_element_type=jnp.float32
        )
        * score_scale
    )
    text_term = jnp.concatenate(
        [grad_text_keys.reshape(TEXT_LEN, D), grad_text_values.reshape(TEXT_LEN, D)], axis=-1
    )[None]
    grad_text_kv = lax.psum_scatter(
        text_term.astype(jnp.bfloat16), "txt", scatter_dimension=1, tiled=True
    )
    cross_kv_grad = weight_grad(text_states, grad_text_kv)
    text_grad = back_project(grad_text_kv, w_cross_kv)
    cross_q_grad = weight_grad(normed2, grad_cross_queries)
    grad_hidden1, norm2_gain_grad, norm2_bias_grad = norm2_back(
        back_project(grad_cross_queries, w_cross_q)
    )
    grad_hidden1 = grad_hidden1 + grad_hidden2
    branch1 = grad_hidden1.astype(jnp.bfloat16)
    self_out_grad = weight_grad(attended, branch1)
    flat_grad_attended = back_project(branch1, w_self_out).astype(jnp.bfloat16)
    grad_attended = flat_grad_attended.reshape(batch_items, local_len, HEADS, HEAD)
    attention = jnp.exp(self_scores() - self_lse)
    grad_attention = jnp.einsum(
        "ilhe,imhe->ihlm", grad_attended, value_rows, preferred_element_type=jnp.float32
    )
    row_delta = jnp.sum(attention * grad_attention, axis=-1, keepdims=True)
    self_score_grad = (attention * (grad_attention - row_delta)).astype(jnp.bfloat16)
    grad_queries = (
        jnp.einsum("ihlm,imhe->ilhe", self_score_grad, key_rows, preferred_element_type=jnp.float32)
        * score_scale
    )
    grad_queries = grad_queries.astype(jnp.bfloat16).reshape(batch_items, local_len, D)
    grad_values = jnp.einsum(
        "ihlm,ilhe->imhe",
        attention.astype(jnp.bfloat16),
        grad_attended,
        preferred_element_type=jnp.float32,
    )
    grad_keys = (
        jnp.einsum("ihlm,ilhe->imhe", self_score_grad, queries, preferred_element_type=jnp.float32)
        * score_scale
    )
    self_term = jnp.concatenate(
        [
            grad_keys.reshape(batch_items, ITEM_LEN, D),
            grad_values.reshape(batch_items, ITEM_LEN, D),
        ],
        axis=-1,
    )
    grad_self_kv = lax.psum_scatter(
        self_term.astype(jnp.bfloat16), "txt", scatter_dimension=1, tiled=True
    )
    grad_joined = jnp.concatenate([grad_queries, grad_self_kv], axis=-1)
    qkv_grad = weight_grad(normed1, grad_joined)
    grad_tokens, norm1_gain_grad, norm1_bias_grad = norm1_back(back_project(grad_joined, w_qkv))
    image_grad = grad_tokens + grad_hidden1
    summed = (
        lax.psum_scatter(norm3_gain_grad, ("img", "txt"), scatter_dimension=0, tiled=True),
        lax.psum_scatter(norm3_bias_grad, ("img", "txt"), scatter_dimension=0, tiled=True),
        lax.psum_scatter(up_grad, ("img", "txt"), scatter_dimension=0, tiled=True),
        lax.psum_scatter(down_grad, ("img", "txt"), scatter_dimension=0, tiled=True),
        lax.psum_scatter(cross_out_grad, ("img", "txt"), scatter_dimension=0, tiled=True),
        lax.psum_scatter(cross_q_grad, ("img", "txt"), scatter_dimension=0, tiled=True),
        lax.psum_scatter(norm2_gain_grad, ("img", "txt"), scatter_dimension=0, tiled=True),
        lax.psum_scatter(norm2_bias_grad, ("img", "txt"), scatter_dimension=0, tiled=True),
        lax.psum_scatter(norm1_gain_grad, ("img", "txt"), scatter_dimension=0, tiled=True),
        lax.psum_scatter(norm1_bias_grad, ("img", "txt"), scatter_dimension=0, tiled=True),
        lax.psum_scatter(qkv_grad, ("img", "txt"), scatter_dimension=0, tiled=True),
        lax.psum_scatter(self_out_grad, ("img", "txt"), scatter_dimension=0, tiled=True),
        lax.psum_scatter(cross_kv_grad, ("img", "txt"), scatter_dimension=0, tiled=True),
    )
    later_sums = summed[:8]
    first_sums = summed[8:]
    return (
        block_out,
        image_grad,
        text_grad,
        first_sums[0],
        first_sums[1],
        first_sums[2],
        first_sums[3],
        later_sums[6],
        later_sums[7],
        later_sums[5],
        first_sums[4],
        later_sums[4],
        later_sums[0],
        later_sums[1],
        later_sums[2],
        later_sums[3],
    )


def solution(mesh):
    placed = (
        P("img", "txt", None),
        P("img", "txt", None),
        P("img", "txt"),
        P("img", None),
        P(),
        P(),
        P(),
        P(),
        P(),
        P(),
        P(),
        P(),
        P(),
        P(),
        P(),
        P(),
        P(),
        P("img", "txt", None),
    )
    return jax.shard_map(
        per_device,
        mesh=mesh,
        in_specs=placed,
        out_specs=(
            P("img", "txt", None),
            P("img", "txt", None),
            P("img", "txt", None),
            P(("img", "txt")),
            P(("img", "txt")),
            P(("img", "txt"), None),
            P(("img", "txt"), None),
            P(("img", "txt")),
            P(("img", "txt")),
            P(("img", "txt"), None),
            P(("img", "txt"), None),
            P(("img", "txt"), None),
            P(("img", "txt")),
            P(("img", "txt")),
            P(("img", "txt"), None),
            P(("img", "txt"), None),
        ),
        check_vma=False,
    )
```

profile of v0, /device:TPU:0, one launch (start us, length us, event | category | flops | bytes accessed | tf_op | source)
XLA Modules:
  0.0 1530.5 jit_solution(13240579491896180882)
XLA Ops:
  11.1 6.7 fusion.27
  26.5 8.7 all-gather
  40.0 7.4 all-reduce
  47.7 34.6 %all-gather.3.cloned.1.call-done = bf16[2,1024,2048]{2,1,0:T(8,128)(2,1)} async-done(((bf16[2,256,2048]{2,1,0:T(8,128)(2,1)}), bf16[2,1024,2048]{2,1,0:T(8,128)(2,1)}) %all-gather.3.cloned.1.call-update) | async-done | bytes 8388624 | tf_op jit(solution)/shard_map/all_gather | solution.py:79
  100.7 15.9 %fusion.135 = (f32[2,16,256]{2,1,0:T(8,128)S(1)}, f32[2,16,256,1024]{3,2,1,0:T(8,128)}) fusion(bf16[2,256,16,64]{1,3,2,0:T(8,128)(2,1)S(1)} %bitcast.210, bf16[2,1024,16,64]{1,3,2,0:T(8,128)(2,1)} %bitcast.202, pred[256,1024]{1,0:T(8,128)(4,1)S(1)} %iota_compare_fusion), kind=kOutput, calls=%fused_computation.181 | convolution fusion | flops 1098899456 | bytes 39092224 | tf_op jit(solution)/shard_map/ilhe,imhe->ihlm/dot_general | solution.py:86
  116.6 14.3 fusion.1
  131.0 16.0 %fusion.85 = bf16[2,16,64,256]{3,2,1,0:T(8,128)(2,1)} fusion(bf16[2,1024,16,64]{1,3,2,0:T(8,128)(2,1)} %bitcast.204, f32[2,16,256,1024]{3,2,1,0:T(8,128)} %get-tuple-element.110, f32[2,16,256]{2,1,0:T(8,128)S(1)} %fusion.1, f32[2,16,256]{2,1,0:T(8,128)S(1)} %get-tuple-element.109), kind=kOutput, calls=%fused_computation.123 | convolution fusion | flops 1099431936 | bytes 38862848 | tf_op jit(solution)/shard_map/ihlm,imhe->ilhe/dot_general | solution.py:92
  166.0 10.1 fusion.67
  176.1 20.1 %multiply_convert_fusion.2 = (bf16[2,256,4096]{2,1,0:T(8,128)(2,1)}, f32[2,256,4096]{2,1,0:T(8,128)}) fusion(f32[2,256,4096]{2,1,0:T(8,128)S(1)} %get-tuple-element.117, u8[256,4096]{1,0:T(8,128)(4,1)S(1)} %get-tuple-element.81, u8[256,4096]{1,0:T(8,128)(4,1)S(1)} %get-tuple-element.80), kind=kLoop, calls=%fused_computation.32 | loop fusion | flops 146800640 | bytes 23068672 | tf_op jit(solution)/shard_map/convert_element_type | solution.py:131
  196.3 12.3 add_convert_fusion
  208.6 9.3 multiply_reduce_fusion.1
  245.0 15.4 %fusion.38 = bf16[2,16,64,1024]{3,2,1,0:T(8,128)(2,1)} fusion(bf16[2,256,16,64]{1,3,2,0:T(8,128)(2,1)S(1)} %bitcast.208, f32[2,16,256,1024]{3,2,1,0:T(8,128)} %get-tuple-element.110, f32[2,16,256]{2,1,0:T(8,128)S(1)} %log_add_fusion), kind=kOutput, calls=%fused_computation.71 | convolution fusion | flops 1092616192 | bytes 38830080 | tf_op jit(solution)/shard_map/ihlm,ilhe->imhe/dot_general | solution.py:193
  260.4 24.0 %multiply_reduce_fusion = (f32[2,16,256]{2,1,0:T(8,128)S(1)}, f32[2,16,256,1024]{3,2,1,0:T(8,128)}) fusion(f32[2,16,256,1024]{3,2,1,0:T(8,128)} %get-tuple-element.110, f32[2,16,256]{2,1,0:T(8,128)S(1)} %log_add_fusion, bf16[2,256,16,64]{1,3,2,0:T(8,128)(2,1)S(1)} %bitcast.209, bf16[2,1024,16,64]{1,3,2,0:T(8,128)(2,1)} %bitcast.205), kind=kOutput, calls=%fused_computation.2 | convolution fusion | flops 1098899456 | bytes 72417280 | tf_op jit(solution)/shard_map/ilhe,imhe->ihlm/dot_general | solution.py:183
  287.6 6.3 copy.139
  293.9 28.4 %multiply_convert_fusion = bf16[2,16,256,1024]{3,2,1,0:T(8,128)(2,1)} fusion(f32[2,16,256,1024]{3,2,1,0:T(8,128)} %get-tuple-element.123, f32[2,16,256,1024]{3,2,1,0:T(8,128)} %get-tuple-element.110, f32[2,16,256]{2,1,0:T(8,128)S(1)} %get-tuple-element.122, f32[2,16,256]{2,1,0:T(8,128)S(1)} %log_add_fusion), kind=kLoop, calls=%fused_computation.1 | loop fusion | flops 33554432 | bytes 83951616 | tf_op jit(solution)/shard_map/convert_element_type | solution.py:187
  322.3 10.7 multiply_convert_fusion.1
  339.2 8.1 pad_maximum_fusion
  370.1 9.6 copy.164
  381.4 10.6 convolution_bitcast_fusion.1
  393.3 10.5 convolution_bitcast_fusion
  403.8 13.4 multiply_convert_fusion.3
  419.7 8.5 convolution_bitcast_fusion.2
  428.2 10.3 add_convert_fusion.1
  440.5 6.4 fusion.129
  449.3 39.8 %all-reduce.8 = (f32[1024]{0:T(1024)S(1)}, f32[1024]{0:T(1024)S(1)}, f32[1024]{0:T(1024)S(1)}, f32[1024]{0:T(1024)S(1)}, f32[1024]{0:T(1024)S(1)}, /*index=5*/f32[1024]{0:T(1024)S(1)}) all-reduce(f32[1024]{0:T(1024)S(1)} %get-tuple-element.86, f32[1024]{0:T(1024)S(1)} %get-tuple-element.91, ...), channel_id=5, replica_groups=mesh['img'=8,'txt'=4] {'img','txt'}, use_global_device_ids=true, to_apply=%region_21.22.clone | all-reduce | flops 6144 | bytes 49152
  496.9 66.4 %reduce-scatter.19.cloned.1.call-done = f32[32,1024]{1,0:T(8,128)} async-done(((f32[1024,1024]{1,0:T(8,128)}), f32[32,1024]{1,0:T(8,128)}) %reduce-scatter.19.cloned.1.call-update) | async-done | bytes 131088 | tf_op jit(solution)/shard_map/reduce_scatter | solution.py:222
  563.2 140.2 %reduce-scatter.17.cloned.1.call-done = f32[32,1024]{1,0:T(8,128)} async-done(((f32[1024,1024]{1,0:T(8,128)}), f32[32,1024]{1,0:T(8,128)}) %reduce-scatter.17.cloned.1.call-update) | async-done | bytes 131088 | tf_op jit(solution)/shard_map/reduce_scatter | solution.py:223
  703.4 139.8 %reduce-scatter.15.cloned.1.call-done = f32[32,1024]{1,0:T(8,128)} async-done(((f32[1024,1024]{1,0:T(8,128)}), f32[32,1024]{1,0:T(8,128)}) %reduce-scatter.15.cloned.1.call-update) | async-done | bytes 131088 | tf_op jit(solution)/shard_map/reduce_scatter | solution.py:229
  843.2 147.6 %reduce-scatter.25.cloned.1.call-done = f32[32,2048]{1,0:T(8,128)} async-done(((f32[1024,2048]{1,0:T(8,128)}), f32[32,2048]{1,0:T(8,128)}) %reduce-scatter.25.cloned.1.call-update) | async-done | bytes 262160
  990.8 181.8 %reduce-scatter.21.cloned.1.call-done = f32[32,4096]{1,0:T(8,128)} async-done(((f32[1024,4096]{1,0:T(8,128)}), f32[32,4096]{1,0:T(8,128)}) %reduce-scatter.21.cloned.1.call-update) | async-done | bytes 524304 | tf_op jit(solution)/shard_map/reduce_scatter | solution.py:220
  1172.6 187.5 %reduce-scatter.23.cloned.1.call-done = f32[128,1024]{1,0:T(8,128)} async-done(((f32[4096,1024]{1,0:T(8,128)}), f32[128,1024]{1,0:T(8,128)}) %reduce-scatter.23.cloned.1.call-update) | async-done | bytes 524304 | tf_op jit(solution)/shard_map/reduce_scatter | solution.py:221
  1360.1 163.4 %reduce-scatter.13.cloned.1.call-done = f32[32,3072]{1,0:T(8,128)} async-done(((f32[1024,3072]{1,0:T(8,128)}), f32[32,3072]{1,0:T(8,128)}) %reduce-scatter.13.cloned.1.call-update) | async-done | bytes 393232 | tf_op jit(solution)/shard_map/reduce_scatter | solution.py:228
  (231 shorter events, 129.9 us)
Async XLA Ops:
  7.2 145.8 %copy-start = (bf16[1024,1024]{1,0:T(8,128)(2,1)S(1)}, bf16[1024,1024]{1,0:T(8,128)(2,1)}, u32[]{:S(2)}) copy-start(bf16[1024,1024]{1,0:T(8,128)(2,1)} %param.28) | copy-start | bytes 6291460
  7.2 75.2 %all-gather.3.cloned.1.call-start = ((), (), s32[]{:S(2)}) async-start(), calls=%async_computation.8 | async-start | bytes 10485760 | tf_op jit(solution)/shard_map/all_gather | solution.py:79
  8.8 8.9 copy-start.39
  21.1 343.2 %all-reduce.11.cloned.1.call-start = ((), (), s32[]{:S(2)}) async-start(), calls=%async_computation.17 | async-start | bytes 2097152
  23.4 14.9 copy-start.57
  23.4 16.3 %copy-start.62 = (s32[1,32]{1,0:T(1,128)S(1)}, s32[1,32]{1,0:T(1,128)}, u32[]{:S(2)}) copy-start(s32[1,32]{1,0:T(1,128)} %param.20) | copy-start | bytes 388
  23.4 24.0 %copy-start.63 = (s32[1,2]{1,0:T(1,128)S(1)}, s32[1,2]{1,0:T(1,128)}, u32[]{:S(2)}) copy-start(s32[1,2]{1,0:T(1,128)} %param.21) | copy-start | bytes 28
  38.3 62.4 %copy-start.12 = (bf16[2,256,1024]{1,2,0:T(8,128)(2,1)}, bf16[2,256,1024]{1,2,0:T(8,128)(2,1)S(1)}, u32[]{:S(2)}) copy-start(bf16[2,256,1024]{1,2,0:T(8,128)(2,1)S(1)} %copy.122) | copy-start | bytes 3145732
  130.9 16.0 %copy-start.5 = (bf16[2,256,1024]{2,1,0:T(8,128)(2,1)S(1)}, bf16[2,256,1024]{2,1,0:T(8,128)(2,1)}, u32[]{:S(2)}) copy-start(bf16[2,256,1024]{2,1,0:T(8,128)(2,1)} %param.18) | copy-start | bytes 3145732
  165.6 52.3 %copy-start.15 = (f32[2,256,1024]{2,1,0:T(8,128)}, f32[2,256,1024]{2,1,0:T(8,128)S(1)}, u32[]{:S(2)}) copy-start(f32[2,256,1024]{2,1,0:T(8,128)S(1)} %get-tuple-element.116) | copy-start | bytes 6291460
  260.4 24.0 %copy-start.44 = (bf16[16,64,128]{2,1,0:T(8,128)(2,1)S(1)}, bf16[16,64,128]{2,1,0:T(8,128)(2,1)}, u32[]{:S(2)}) copy-start(bf16[16,64,128]{2,1,0:T(8,128)(2,1)} %fusion.101) | copy-start | bytes 786436
  260.4 24.5 %copy-start.45 = (bf16[16,64,128]{2,1,0:T(8,128)(2,1)S(1)}, bf16[16,64,128]{2,1,0:T(8,128)(2,1)}, u32[]{:S(2)}) copy-start(bf16[16,64,128]{2,1,0:T(8,128)(2,1)} %fusion.98) | copy-start | bytes 786436
  287.6 132.1 %reduce-scatter.11.cloned.1.call-start = ((), (), s32[]{:S(2)}) async-start(), calls=%async_computation.9 | async-start | bytes 10485760 | tf_op jit(solution)/shard_map/reduce_scatter | solution.py:210
  293.9 28.4 %copy-start.13 = (bf16[2,256,1024]{1,2,0:T(8,128)(2,1)S(1)}, bf16[2,256,1024]{1,2,0:T(8,128)(2,1)}, u32[]{:S(2)}) copy-start(bf16[2,256,1024]{1,2,0:T(8,128)(2,1)} %copy-done.12) | copy-start | bytes 3145732
  347.4 215.8 %reduce-scatter.19.cloned.1.call-start = ((), (), s32[]{:S(2)}) async-start(), calls=%async_computation.13 | async-start | bytes 4325376 | tf_op jit(solution)/shard_map/reduce_scatter | solution.py:222
  352.1 351.3 %reduce-scatter.17.cloned.1.call-start = ((), (), s32[]{:S(2)}) async-start(), calls=%async_computation.12 | async-start | bytes 4325376 | tf_op jit(solution)/shard_map/reduce_scatter | solution.py:223
  357.9 485.3 %reduce-scatter.15.cloned.1.call-start = ((), (), s32[]{:S(2)}) async-start(), calls=%async_computation.11 | async-start | bytes 4325376 | tf_op jit(solution)/shard_map/reduce_scatter | solution.py:229
  363.6 627.2 %reduce-scatter.25.cloned.1.call-start = ((), (), s32[]{:S(2)}) async-start(), calls=%async_computation.16 | async-start | bytes 8650752
  379.7 792.9 %reduce-scatter.21.cloned.1.call-start = ((), (), s32[]{:S(2)}) async-start(), calls=%async_computation.14 | async-start | bytes 17301504 | tf_op jit(solution)/shard_map/reduce_scatter | solution.py:220
  392.1 968.1 %reduce-scatter.23.cloned.1.call-start = ((), (), s32[]{:S(2)}) async-start(), calls=%async_computation.15 | async-start | bytes 17301504 | tf_op jit(solution)/shard_map/reduce_scatter | solution.py:221
  403.7 15.9 %copy-start.6 = (bf16[2,256,1024]{2,1,0:T(8,128)(2,1)S(1)}, bf16[2,256,1024]{2,1,0:T(8,128)(2,1)}, u32[]{:S(2)}) copy-start(bf16[2,256,1024]{2,1,0:T(8,128)(2,1)} %param.18) | copy-start | bytes 3145732
  403.7 15.9 %copy-start.38 = (f32[1024]{0:T(1024)S(1)}, f32[1024]{0:T(1024)}, u32[]{:S(2)}) copy-start(f32[1024]{0:T(1024)} %param.22) | copy-start | bytes 12292
  403.8 15.9 %copy-start.40 = (f32[2,256]{1,0:T(2,128)S(1)}, f32[2,256]{1,0:T(2,128)}, u32[]{:S(2)}) copy-start(f32[2,256]{1,0:T(2,128)} %copy-done.39) | copy-start | bytes 6148
  403.8 15.9 %copy-start.43 = (f32[1024]{0:T(1024)S(1)}, f32[1024]{0:T(1024)}, u32[]{:S(2)}) copy-start(f32[1024]{0:T(1024)} %param.23) | copy-start | bytes 12292
  403.8 15.9 %copy-start.47 = (f32[2,256]{1,0:T(2,128)S(1)}, f32[2,256]{1,0:T(2,128)}, u32[]{:S(2)}) copy-start(f32[2,256]{1,0:T(2,128)} %copy-done.46) | copy-start | bytes 6148
  403.8 1119.7 %reduce-scatter.13.cloned.1.call-start = ((), (), s32[]{:S(2)}) async-start(), calls=%async_computation.10 | async-start | bytes 12976128 | tf_op jit(solution)/shard_map/reduce_scatter | solution.py:228
  428.2 10.3 copy-start.9
  440.5 8.8 copy-start.51
  440.5 8.8 copy-start.53
  440.5 8.8 copy-start.54
  440.5 8.8 copy-start.55
  448.3 1075.2 %copy-start.1 = (bf16[1024,1024]{1,0:T(8,128)(2,1)S(1)}, bf16[1024,1024]{1,0:T(8,128)(2,1)}, u32[]{:S(2)}) copy-start(bf16[1024,1024]{1,0:T(8,128)(2,1)} %param.28) | copy-start | bytes 6291460
  (42 other events, 108.4 us)
Sparse Core Ops, SparseCore 0:
  21.2 61.1 all-gather.2
  287.7 36.0 all-reduce.10
  347.5 71.6 reduce-scatter.10
  421.9 141.2 reduce-scatter.18
  565.9 137.4 reduce-scatter.16
  706.1 137.0 reduce-scatter.14
  846.1 144.6 reduce-scatter.24
  993.7 178.9 reduce-scatter.20
  1175.5 184.5 reduce-scatter.22
  1366.6 156.8 reduce-scatter.12
where the time goes:
time: 1540 us; the launch traced here: 1530 us
  waiting for transfers between devices  1060 us (69%)
  matrix products  223 us (14%)
  other arithmetic  90.1 us (6%)
  local copies, waits for them, and re-layouts  82.6 us (5%)
  blocking collectives  55.9 us (4%)
  between operations  16.5 us (1%)
    reduce_scatter x1, waiting for transfers between devices, per_device(): lax.psum_scatter(down_grad, ('img', 'txt'), scatter_dimension=0, tiled=True)  187 us
    reduce_scatter x1, waiting for transfers between devices, per_device(): lax.psum_scatter(up_grad, ('img', 'txt'), scatter_dimension=0, tiled=True)  182 us
    reduce_scatter x1, waiting for transfers between devices, per_device(): lax.psum_scatter(qkv_grad, ('img', 'txt'), scatter_dimension=0, tiled=True)  163 us
    unnamed x12, waiting for transfers between devices  148 us
    reduce_scatter x1, waiting for transfers between devices, per_device(): lax.psum_scatter(cross_q_grad, ('img', 'txt'), scatter_dimension=0, tiled...  140 us
    reduce_scatter x1, waiting for transfers between devices, per_device(): lax.psum_scatter(self_out_grad, ('img', 'txt'), scatter_dimension=0, tile...  140 us
    reduce_scatter x1, waiting for transfers between devices, per_device(): lax.psum_scatter(cross_out_grad, ('img', 'txt'), scatter_dimension=0, til...  66.4 us
    unnamed x2, blocking collectives  47.2 us
  transfers between devices with their start and end apart: 10, of which 8 were waited for; matrix products, arithmetic and copies ran while one was open for 11% of the time, Pallas kernels for 0%

commit v1 on v0

v1 whole, which is shorter than its diff:
```python
from functools import partial

import jax
import jax.numpy as jnp
import numpy as np
from jax import lax
from jax.experimental import pallas as pl
from jax.experimental.pallas import tpu as pltpu
from jax.sharding import PartitionSpec as P

D = 1024
HEADS = 16
HEAD = 64
EPS = 1e-05
MASKED = -1e30
SCALE = HEAD**-0.5
LOG2E = 1.4426950408889634
BOTH = ("img", "txt")
BF = jnp.bfloat16
F32 = jnp.float32
QUERY_BLOCK = 256
MIB = 1 << 20


def nn(a, b):
    return lax.dot_general(a, b, (((1,), (0,)), ((), ())), preferred_element_type=F32)


def nt(a, b):
    return lax.dot_general(a, b, (((1,), (1,)), ((), ())), preferred_element_type=F32)


def tn(a, b):
    return lax.dot_general(a, b, (((0,), (0,)), ((), ())), preferred_element_type=F32)


def norm_parts(values):
    center = values - jnp.mean(values, axis=-1, keepdims=True)
    rstd = lax.rsqrt(jnp.mean(center * center, axis=-1, keepdims=True) + EPS)
    return center * rstd, rstd


def norm_back(unit, rstd, gain, grad):
    scaled = grad * gain
    return rstd * (
        scaled
        - jnp.mean(scaled, axis=-1, keepdims=True)
        - unit * jnp.mean(scaled * unit, axis=-1, keepdims=True)
    )


def gelu_parts(value):
    inner = jnp.clip(value * (0.5**0.5), -4.0, 4.0)
    square = inner * inner
    top = jnp.full_like(square, -2.72614225801306e-10)
    for term in (
        2.77068142495902e-08,
        -2.10102402082508e-06,
        -5.69250639462346e-05,
        -7.34990630326855e-04,
        -2.95459980854025e-03,
        -1.60960333262415e-02,
    ):
        top = top * square + term
    low = jnp.full_like(square, -1.45660718464996e-05)
    for term in (
        -2.13374055278905e-04,
        -1.68282697438203e-03,
        -7.37332916720468e-03,
        -1.42647390514189e-02,
    ):
        low = low * square + term
    cdf = 0.5 + 0.5 * inner * top / low
    density = jnp.exp2(value * value * (-0.5 * LOG2E)) * (0.5 / np.pi) ** 0.5
    return value * cdf, cdf + value * density


def attend_kernel(q_ref, k_ref, v_ref, out_ref, lse_ref):
    length = q_ref.shape[0]
    block = QUERY_BLOCK
    scale = SCALE * LOG2E
    half = lax.broadcasted_iota(jnp.int32, (block, 2 * HEAD), 1) >= HEAD
    key_row = lax.broadcasted_iota(jnp.int32, (block, block), 0)
    query_col = lax.broadcasted_iota(jnp.int32, (block, block), 1)
    seen = key_row <= query_col
    v_flip = v_ref[...].T
    ones = jnp.ones((16, length), BF)
    v_rows = [jnp.concatenate([v_flip[h * HEAD : (h + 1) * HEAD], ones], 0) for h in range(2)]
    for i in range(length // block):
        lo, hi = i * block, (i + 1) * block
        queries = q_ref[lo:hi, :]
        outs = []
        for h in range(2):
            own = jnp.where(half == (h == 1), queries, jnp.zeros_like(queries))
            diag = jnp.where(seen, nt(k_ref[lo:hi, :], own), MASKED)
            top = jnp.max(diag, axis=0, keepdims=True)
            if i:
                rest = nt(k_ref[:lo, :], own)
                top = jnp.maximum(top, jnp.max(rest, axis=0, keepdims=True))
            base = top * scale
            mixed = nn(v_rows[h][:, lo:hi], jnp.exp2(diag * scale - base).astype(BF))
            if i:
                mixed += nn(v_rows[h][:, :lo], jnp.exp2(rest * scale - base).astype(BF))
            total = mixed[HEAD : HEAD + 1]
            lse_ref[0, h : h + 1, lo:hi] = base + jnp.log2(total)
            outs.append(mixed[:HEAD] / total)
        out_ref[lo:hi, :] = jnp.concatenate(outs, 0).T.astype(BF)


def attend(q, k, v):
    length, width = q.shape
    pairs = width // (2 * HEAD)
    spec = pl.BlockSpec((length, 2 * HEAD), lambda p: (0, p))
    return pl.pallas_call(
        attend_kernel,
        grid=(pairs,),
        in_specs=[spec] * 3,
        out_specs=[spec, pl.BlockSpec((1, 2, length), lambda p: (p, 0, 0))],
        out_shape=[
            jax.ShapeDtypeStruct((length, width), BF),
            jax.ShapeDtypeStruct((pairs, 2, length), F32),
        ],
        compiler_params=pltpu.CompilerParams(vmem_limit_bytes=48 * MIB),
        cost_estimate=pl.CostEstimate(
            flops=4 * length * length * width, bytes_accessed=8 * length * width, transcendentals=0
        ),
        name="self_attention",
    )(q, k, v)


def attend_back_kernel(q_ref, k_ref, v_ref, g_ref, o_ref, lse_ref, dq_ref, dk_ref, dv_ref, dq_sum):
    length = q_ref.shape[0]
    block = QUERY_BLOCK
    scale = SCALE * LOG2E
    half = lax.broadcasted_iota(jnp.int32, (length, 2 * HEAD), 1) >= HEAD
    key_row = lax.broadcasted_iota(jnp.int32, (block, block), 0)
    query_col = lax.broadcasted_iota(jnp.int32, (block, block), 1)
    seen = key_row <= query_col
    k_flip = k_ref[...].T
    zero = jnp.zeros((length, 2 * HEAD), BF)
    queries = [jnp.where(half == (h == 1), q_ref[...], zero) for h in range(2)]
    grads = [jnp.where(half == (h == 1), g_ref[...], zero) for h in range(2)]
    product = (g_ref[...].astype(F32) * o_ref[...].astype(F32)).T
    deltas = [jnp.sum(product[h * HEAD : (h + 1) * HEAD], axis=0, keepdims=True) for h in range(2)]
    for j in range(length // block):
        lo, hi = j * block, (j + 1) * block
        keys, values = k_ref[lo:hi, :], v_ref[lo:hi, :]
        key_grad = value_grad = None
        for h in range(2):
            own_q, own_g = queries[h][lo:], grads[h][lo:]
            scores = nt(keys, own_q) * scale - lse_ref[0, h : h + 1, lo:]
            weights = jnp.exp2(scores)
            first = jnp.where(seen, weights[:, :block], 0.0)
            weights = jnp.concatenate([first, weights[:, block:]], 1) if hi < length else first
            score_grad = (weights * (nt(values, own_g) - deltas[h][:, lo:])).astype(BF)
            weights = weights.astype(BF)
            value_part = nn(weights, own_g)
            key_part = nn(score_grad, own_q)
            value_grad = value_part if h == 0 else value_grad + value_part
            key_grad = key_part if h == 0 else key_grad + key_part
            query_part = nn(k_flip[h * HEAD : (h + 1) * HEAD, lo:hi], score_grad)
            rows = slice(h * HEAD, (h + 1) * HEAD)
            if j == 0:
                dq_sum[rows, :] = query_part
            else:
                dq_sum[rows, lo:] += query_part
        dk_ref[lo:hi, :] = (key_grad * SCALE).astype(BF)
        dv_ref[lo:hi, :] = value_grad.astype(BF)
    dq_ref[...] = (dq_sum[...].T * SCALE).astype(BF)


def attend_back(q, k, v, g, o, lse):
    length, width = q.shape
    pairs = width // (2 * HEAD)
    spec = pl.BlockSpec((length, 2 * HEAD), lambda p: (0, p))
    return pl.pallas_call(
        attend_back_kernel,
        grid=(pairs,),
        in_specs=[spec] * 5 + [pl.BlockSpec((1, 2, length), lambda p: (p, 0, 0))],
        out_specs=[spec] * 3,
        out_shape=[jax.ShapeDtypeStruct((length, width), BF)] * 3,
        scratch_shapes=[pltpu.VMEM((2 * HEAD, length), F32)],
        compiler_params=pltpu.CompilerParams(vmem_limit_bytes=48 * MIB),
        cost_estimate=pl.CostEstimate(
            flops=10 * length * length * width, bytes_accessed=16 * length * width, transcendentals=0
        ),
        name="self_attention_back",
    )(q, k, v, g, o, lse)


def mlp_kernel(
    pieces,
    core_ref,
    rows_from,
    goes_to,
    own_ref,
    other_ref,
    own_g_ref,
    other_g_ref,
    *refs,
):
    ups, downs = refs[:pieces], refs[pieces : 2 * pieces]
    out_ref, norm_ref, sent_ref, keep, send = refs[2 * pieces : 2 * pieces + 5]
    flip_ref, ordered_ref, out_sum, norm_sum, wide_ref, tall_ref, sems = refs[2 * pieces + 5 :]
    step, steps = pl.program_id(0), pl.num_programs(0)
    slot = step % 2
    tokens = own_ref.shape[0]
    half, height = keep.shape[0], keep.shape[1]
    tile = wide_ref.shape[3]
    width = 2 * height
    per_step = tile // width
    units = steps * tile

    @pl.when(step == 0)
    def _():
        flip_ref[:, :tokens] = own_ref[...].T
        flip_ref[:, tokens:] = other_ref[...].T
        for i in range(2 * half):
            at = pl.multiple_of(rows_from[i] * height, height)
            ordered_ref[i * height : (i + 1) * height, :] = flip_ref[pl.ds(at, height), :]
        out_ref[...] = jnp.zeros_like(out_ref)
        norm_ref[...] = jnp.zeros_like(norm_ref)
        out_sum[...] = jnp.zeros_like(out_sum)
        norm_sum[...] = jnp.zeros_like(norm_sum)

    def wide_copy(at, where, side):
        part = wide_ref.at[at, side * half : (side + 1) * half]
        lanes = pl.ds(pl.multiple_of(where * tile, tile), tile)
        return pltpu.make_async_copy(
            part, (keep, send)[side].at[:, :, lanes], sems.at[at, side]
        )

    def tall_copy(at, j, r, target, i):
        rows = slice(j * width + r * height, j * width + (r + 1) * height)
        lanes = slice(units + r * D, units + (r + 1) * D)
        return pltpu.make_async_copy(
            tall_ref.at[at, rows], target.at[i, :, lanes], sems.at[at, 2 + 2 * j + r]
        )

    def wait(at):
        for side in range(2):
            wide_copy(at, 0, side).wait()
        for j in range(per_step):
            for r in range(2):
                tall_copy(at, j, r, keep, 0).wait()

    @pl.when(step >= 2)
    def _():
        wait(slot)

    up_w = jnp.concatenate([r[...] for r in ups], 1) if pieces > 1 else ups[0][...]
    down_w = jnp.concatenate([r[...] for r in downs], 0) if pieces > 1 else downs[0][...]
    chunk = min(256, tokens)
    active, grads = [], []
    for x_ref, g_ref, o_ref, n_ref in (
        (own_ref, own_g_ref, out_ref, norm_ref),
        (other_ref, other_g_ref, out_sum, norm_sum),
    ):
        for at in range(0, tokens, chunk):
            rows = slice(at, at + chunk)
            up_value = nn(x_ref[rows, :], up_w)
            down_grad = nt(g_ref[rows, :], down_w)
            value, slope = gelu_parts(up_value)
            value = value.astype(BF)
            grad = (down_grad * slope).astype(BF)
            o_ref[rows, :] += nn(value, down_w)
            n_ref[rows, :] += nt(grad, up_w)
            active.append(value)
            grads.append(grad)
    grad = jnp.concatenate(grads, 0)
    wide = nn(ordered_ref[...], grad).astype(BF)
    wide_ref[slot] = wide.reshape(wide_ref.shape[1:])
    value = jnp.concatenate(active, 0).T
    tall = nn(value[:, :tokens], own_g_ref[...]) + nn(value[:, tokens:], other_g_ref[...])
    tall_ref[slot] = tall.astype(BF)

    for side in range(2):
        wide_copy(slot, step, side).start()
    for j in range(per_step):
        i = goes_to[step * per_step + j]

        @pl.when(i < half)
        def _(j=j, i=i):
            for r in range(2):
                tall_copy(slot, j, r, keep, i).start()

        @pl.when(i >= half)
        def _(j=j, i=i):
            for r in range(2):
                tall_copy(slot, j, r, send, i - half).start()

    @pl.when(step == steps - 1)
    def _():
        sent_ref[0] = out_sum[...].astype(BF)
        sent_ref[1] = norm_sum[...].astype(BF)
        wait(1 - slot)
        wait(slot)


def mlp(own, other, own_g, other_g, w_up, w_down, core, rows_from, goes_to):
    tokens = own.shape[0]
    chips = rows_from.shape[0]
    tile = 256
    units = w_up.shape[1] // 2
    steps = units // tile
    width = units // chips
    height = D // chips
    if width % 128 == 0:
        pieces, piece = tile // width, width
    else:
        pieces, piece = 1, tile
        w_up = w_up.reshape(D, chips, 2, width)[:, :, core].reshape(D, units)
        w_down = w_down.reshape(chips, 2, width, D)[:, core].reshape(units, D)

    def place(s, c, j):
        return 2 * (s * pieces + j) + c[0] if width % 128 == 0 else s

    whole = pl.BlockSpec((tokens, D), lambda s, *_: (0, 0))
    up_specs = [
        pl.BlockSpec((D, piece), lambda s, c, *_, j=j: (0, place(s, c, j))) for j in range(pieces)
    ]
    down_specs = [
        pl.BlockSpec((piece, D), lambda s, c, *_, j=j: (place(s, c, j), 0)) for j in range(pieces)
    ]
    sums = jax.ShapeDtypeStruct((chips // 2, height, units + 2 * D), BF)
    return pl.pallas_call(
        partial(mlp_kernel, pieces),
        grid_spec=pltpu.PrefetchScalarGridSpec(
            num_scalar_prefetch=3,
            grid=(steps,),
            in_specs=[whole] * 4 + up_specs + down_specs,
            out_specs=[
                whole,
                whole,
                pl.BlockSpec((2, tokens, D), lambda s, *_: (0, 0, 0)),
                pl.BlockSpec(memory_space=pl.ANY),
                pl.BlockSpec(memory_space=pl.ANY),
            ],
            scratch_shapes=[
                pltpu.VMEM((D, 2 * tokens), BF),
                pltpu.VMEM((D, 2 * tokens), BF),
                pltpu.VMEM((tokens, D), F32),
                pltpu.VMEM((tokens, D), F32),
                pltpu.VMEM((2, chips, height, tile), BF),
                pltpu.VMEM((2, tile, D), BF),
                pltpu.SemaphoreType.DMA((2, 2 + 2 * (tile // width))),
            ],
        ),
        out_shape=[
            jax.ShapeDtypeStruct((tokens, D), F32),
            jax.ShapeDtypeStruct((tokens, D), F32),
            jax.ShapeDtypeStruct((2, tokens, D), BF),
            sums,
            sums,
        ],
        compiler_params=pltpu.CompilerParams(vmem_limit_bytes=56 * MIB),
        cost_estimate=pl.CostEstimate(
            flops=24 * tokens * D * units, bytes_accessed=12 * D * units, transcendentals=0
        ),
        name="mlp_both_ways",
    )(
        core.reshape(1),
        rows_from,
        goes_to,
        own,
        other,
        own_g,
        other_g,
        *([w_up] * pieces),
        *([w_down] * pieces),
    )


class Plan:
    def __init__(self, n_img, n_txt):
        self.n_txt = n_txt
        self.n = n_img * n_txt
        self.chips = self.n // 2
        self.ny = n_txt // 2
        self.levels = self.chips.bit_length() - 1
        rest = list(range(2, self.levels))
        self.orders = ([1, 0] + rest, [0, 1] + rest)
        self.me = lax.axis_index("img") * n_txt + lax.axis_index("txt")
        self.core = self.me % 2
        self.chip = self.me // 2
        self.y = lax.axis_index("txt") // 2
        maps = np.zeros((2, self.chips), np.int32)
        for core in range(2):
            for i in range(self.chips):
                for s, bit in enumerate(self.orders[core]):
                    maps[core, i] |= ((i >> (self.levels - 1 - s)) & 1) << bit
        self.blocks = jnp.bitwise_xor(
            self.chip, jnp.where(self.core == 0, jnp.asarray(maps[0]), jnp.asarray(maps[1]))
        ).astype(jnp.int32)
        backs = np.argsort(maps, axis=1).astype(np.int32)
        away = jnp.bitwise_xor(self.chip, jnp.arange(self.chips, dtype=jnp.int32))
        self.goes_to = jnp.take(jnp.asarray(backs)[self.core], away, mode="clip")

    def swap(self, value):
        return lax.ppermute(value, BOTH, [(d, d ^ 1) for d in range(self.n)])

    def shift_y(self, value, by):
        pairs = []
        for d in range(self.n):
            img, txt = divmod(d, self.n_txt)
            y, core = divmod(txt, 2)
            pairs.append((d, img * self.n_txt + ((y + by) % self.ny) * 2 + core))
        return lax.ppermute(value, BOTH, pairs)

    def halve(self, value, step):
        pairs = [(d, d ^ (2 << self.orders[d % 2][step])) for d in range(self.n)]
        return lax.ppermute(value, BOTH, pairs)

    def to_item(self, value):
        parts = [value[self.y]]
        for k in range(1, self.ny):
            parts.append(self.shift_y(value[(self.y + k) % self.ny], k))
        return jnp.stack(parts)

    def from_item(self, value):
        parts = [value[0]]
        for k in range(1, self.ny):
            parts.append(self.shift_y(value[k], -k))
        stacked = jnp.stack(parts)
        order = [(i - self.y) % self.ny for i in range(self.ny)]
        return jnp.stack([stacked[o] for o in order])

    def to_places(self, own, other):
        length = own.shape[0] // self.ny
        both = jnp.concatenate([own, other], 0).reshape(2 * self.ny, length, -1)
        order = [
            ((p % 2) ^ self.core) * self.ny + (self.y - p // 2) % self.ny for p in range(self.n_txt)
        ]
        return jnp.concatenate([both[o] for o in order], 0)

    def from_places(self, value):
        length = value.shape[0] // self.n_txt
        parts = value.reshape(self.n_txt, length, -1)
        own = [parts[((self.y - r) % self.ny) * 2 + self.core] for r in range(self.ny)]
        other = [parts[((self.y - r) % self.ny) * 2 + 1 - self.core] for r in range(self.ny)]
        return jnp.concatenate(own, 0), jnp.concatenate(other, 0)

    def reduce(self, keep, send):
        for s in range(self.levels):
            got = [self.halve(v, s) for v in send]
            total = [a.astype(F32) + b.astype(F32) for a, b in zip(keep, got, strict=True)]
            if s < self.levels - 1:
                half = total[0].shape[0] // 2
                keep = [t[:half].astype(BF) for t in total]
                send = [t[half:].astype(BF) for t in total]
        return [t[0] for t in total]

    def split(self, value):
        ordered = jnp.take(value, self.blocks, axis=0, mode="clip")
        return ordered[: self.chips // 2], ordered[self.chips // 2 :]


def per_device(
    n_img,
    n_txt,
    image_tokens,
    text_states,
    text_segments,
    item_segments,
    norm1_gain,
    norm1_bias,
    w_qkv,
    w_self_out,
    norm2_gain,
    norm2_bias,
    w_cross_q,
    w_cross_kv,
    w_cross_out,
    norm3_gain,
    norm3_bias,
    w_up,
    w_down,
    cotangent,
):
    plan = Plan(n_img, n_txt)
    core, n, chips, ny = plan.core, plan.n, plan.chips, plan.ny
    items, length, _ = image_tokens.shape
    tokens = items * length
    half_d = D // 2
    rows = D // n

    x_own = plan.to_item(image_tokens).reshape(tokens, D)
    g_own = plan.to_item(cotangent).reshape(tokens, D)
    x_other = plan.swap(x_own)
    g_other = plan.swap(g_own)
    x_all = jnp.concatenate([x_own, x_other], 0)

    states = lax.all_gather(text_states[0], "txt", axis=0, tiled=True)
    ids = lax.all_gather(text_segments[0].astype(BF), "txt", axis=0, tiled=True)
    text_kv = nn(states, w_cross_kv).astype(BF)

    unit1_all, rstd1_all = norm_parts(x_all.astype(F32))
    normed1 = (unit1_all * norm1_gain + norm1_bias).astype(BF)
    w_own = [lax.dynamic_slice(w_qkv, (0, s * D + core * half_d), (D, half_d)) for s in range(3)]
    w_own = jnp.concatenate(w_own, 1)
    joined = nn(normed1, w_own).astype(BF)
    placed = plan.to_places(joined[:tokens], joined[tokens:])
    q, k, v = placed[:, :half_d], placed[:, half_d : 2 * half_d], placed[:, 2 * half_d :]
    mixed, lse = attend(q, k, v)
    mixed_own, mixed_other = plan.from_places(mixed)
    mixed_got = plan.swap(mixed_other)
    attended = jnp.where(
        core == 0,
        jnp.concatenate([mixed_own, mixed_got], 1),
        jnp.concatenate([mixed_got, mixed_own], 1),
    )

    hidden1 = x_own.astype(F32) + nn(attended, w_self_out)
    unit2, rstd2 = norm_parts(hidden1)
    normed2 = (unit2 * norm2_gain + norm2_bias).astype(BF)
    cross_q = nn(normed2, w_cross_q).astype(BF)
    cq = cross_q.reshape(tokens, HEADS, HEAD)
    tk = text_kv[:, :D].reshape(-1, HEADS, HEAD)
    tv = text_kv[:, D:].reshape(-1, HEADS, HEAD)
    matches = ids == item_segments[0, plan.y].astype(BF)
    scores = jnp.einsum("lhe,she->hls", cq, tk, preferred_element_type=F32) * SCALE
    scores = jnp.where(matches[None, None, :], scores, MASKED)
    weights = jnp.exp(scores - jnp.max(scores, axis=-1, keepdims=True))
    weights = weights / jnp.sum(weights, axis=-1, keepdims=True)
    weights_low = weights.astype(BF)
    cross_mixed = jnp.einsum("hls,she->lhe", weights_low, tv, preferred_element_type=F32)
    cross_mixed = cross_mixed.reshape(tokens, D).astype(BF)
    hidden2 = hidden1 + nn(cross_mixed, w_cross_out)
    unit3, rstd3 = norm_parts(hidden2)
    normed3 = (unit3 * norm3_gain + norm3_bias).astype(BF)

    normed3_other = plan.swap(normed3)
    per_down = w_down.shape[0] // n
    out, grad3, sent, up_down_keep, up_down_send = mlp(
        normed3, normed3_other, g_own, g_other, w_up, w_down, core, plan.blocks, plan.goes_to
    )
    got = plan.swap(sent).astype(F32)
    block_out = (hidden2 + out + got[0]).astype(BF)
    grad3 = grad3 + got[1]
    (up_down,) = plan.reduce([up_down_keep], [up_down_send])

    block_out = plan.from_item(block_out.reshape(ny, length, D))

    grad_gain3 = jnp.sum(grad3 * unit3, axis=0)
    grad_bias3 = jnp.sum(grad3, axis=0)
    grad_hidden2 = norm_back(unit3, rstd3, norm3_gain, grad3) + g_own.astype(F32)
    branch2 = grad_hidden2.astype(BF)
    cross_out_grad = tn(cross_mixed, branch2)
    grad_mixed = nt(branch2, w_cross_out).astype(BF).reshape(tokens, HEADS, HEAD)
    grad_weights = jnp.einsum("lhe,she->hls", grad_mixed, tv, preferred_element_type=F32)
    grad_tv = jnp.einsum("hls,lhe->she", weights_low, grad_mixed, preferred_element_type=F32)
    grad_scores = weights * (
        grad_weights - jnp.sum(weights * grad_weights, axis=-1, keepdims=True)
    )
    grad_scores = grad_scores.astype(BF)
    grad_cq = jnp.einsum("hls,she->lhe", grad_scores, tk, preferred_element_type=F32) * SCALE
    grad_cq = grad_cq.astype(BF).reshape(tokens, D)
    grad_tk = jnp.einsum("hls,lhe->she", grad_scores, cq, preferred_element_type=F32) * SCALE
    grad_kv = jnp.concatenate([grad_tk.reshape(-1, D), grad_tv.reshape(-1, D)], 1).astype(BF)
    cross_kv_grad = tn(states, grad_kv)
    text_part = nt(grad_kv, w_cross_kv)
    text_grad = lax.psum_scatter(text_part.astype(BF), "txt", scatter_dimension=0, tiled=True)
    cross_q_grad = tn(normed2, grad_cq)
    grad2 = nt(grad_cq, w_cross_q)
    grad_gain2 = jnp.sum(grad2 * unit2, axis=0)
    grad_bias2 = jnp.sum(grad2, axis=0)
    grad_hidden1 = norm_back(unit2, rstd2, norm2_gain, grad2) + grad_hidden2
    branch1 = grad_hidden1.astype(BF)
    self_out_grad = tn(attended, branch1)
    middle = jnp.concatenate([cross_out_grad, cross_q_grad, self_out_grad, cross_kv_grad], 1)
    middle = middle.astype(BF).reshape(chips, 2, rows, -1)
    middle = middle[:, core].astype(F32) + plan.swap(middle[:, 1 - core]).astype(F32)
    mid_keep, mid_send = plan.split(middle.astype(BF))
    (mid_sums,) = plan.reduce([mid_keep], [mid_send])

    grad_attended = nt(branch1, w_self_out).astype(BF).reshape(tokens, 2, half_d)
    grad_got = plan.swap(grad_attended[:, 1 - core])
    grad_placed = plan.to_places(grad_attended[:, core], grad_got)
    dq, dk, dv = attend_back(q, k, v, grad_placed, mixed, lse)
    joined_own, joined_other = plan.from_places(jnp.concatenate([dq, dk, dv], 1))
    joined_grad = jnp.concatenate([joined_own, joined_other], 0)
    part1 = nt(joined_grad, w_own)
    grad1 = part1[:tokens] + plan.swap(part1[tokens:].astype(BF)).astype(F32)
    qkv_grad = tn(normed1, joined_grad)
    unit1, rstd1 = unit1_all[:tokens], rstd1_all[:tokens]
    grad_gain1 = jnp.sum(grad1 * unit1, axis=0)
    grad_bias1 = jnp.sum(grad1, axis=0)
    norms = jnp.stack([grad_gain1, grad_bias1, grad_gain2, grad_bias2, grad_gain3, grad_bias3])
    norms = norms.reshape(6, chips, 2 * rows).transpose(1, 2, 0).astype(BF)
    norms = jnp.pad(norms, ((0, 0), (0, 0), (0, 128 - 6)))
    last = jnp.concatenate([qkv_grad.astype(BF).reshape(chips, 2 * rows, -1), norms], -1)
    last_keep, last_send = plan.split(last)
    (last_sums,) = plan.reduce([last_keep], [last_send])

    image_grad = norm_back(unit1, rstd1, norm1_gain, grad1) + grad_hidden1
    image_grad = plan.from_item(image_grad.astype(BF).reshape(ny, length, D)).astype(F32)

    units = w_up.shape[1] // 2
    down_grad = jnp.concatenate([up_down[:, units : units + D], up_down[:, units + D :]], 0)
    parts = jnp.concatenate([up_down[:, :units], last_sums], 1).reshape(2, rows, -1)
    mine = parts[core]
    theirs = plan.swap(parts[1 - core].astype(BF)).astype(F32)
    by_core = jnp.where(core == 0, jnp.stack([mine, theirs]), jnp.stack([theirs, mine]))
    up_grad = by_core[:, :, :units].reshape(2, rows, chips, per_down)
    up_grad = up_grad.transpose(1, 2, 0, 3).reshape(rows, 2 * units)
    wide = by_core[:, :, units : units + 3 * half_d].reshape(2, rows, 3, half_d)
    wide = wide.transpose(1, 2, 0, 3).reshape(rows, 3 * D)
    norm_sums = mine[:, -128:-122] + theirs[:, -128:-122]
    return (
        block_out,
        image_grad,
        text_grad.astype(F32)[None],
        norm_sums[:, 0],
        norm_sums[:, 1],
        wide,
        mid_sums[:, 2 * D : 3 * D],
        norm_sums[:, 2],
        norm_sums[:, 3],
        mid_sums[:, D : 2 * D],
        mid_sums[:, 3 * D :],
        mid_sums[:, :D],
        norm_sums[:, 4],
        norm_sums[:, 5],
        up_grad,
        down_grad,
    )


def solution(mesh):
    split = P("img", "txt", None)
    rows = P(BOTH)
    wide = P(BOTH, None)
    return jax.shard_map(
        partial(per_device, mesh.shape["img"], mesh.shape["txt"]),
        mesh=mesh,
        in_specs=(split, split, P("img", "txt"), P("img", None)) + (P(),) * 13 + (split,),
        out_specs=(
            (split,) * 3
            + (rows, rows, wide, wide)
            + (rows, rows, wide, wide, wide)
            + (rows, rows, wide, wide)
        ),
        check_vma=False,
    )
```

time: 1540 us -> 487 us (0.32)
  waiting for transfers between devices: 1060 us -> 131 us
  matrix products: 223 us -> 59.4 us
  Pallas kernels: 0 us -> 80.9 us
  blocking collectives: 55.9 us -> 21.7 us
  starting transfers between devices: 0.82 us -> 25.1 us
    reduce_scatter x7 -> x1, waiting for transfers between devices: 879 us -> 0.01 us  [per_device(): lax.psum_scatter(text_part.astype(BF), 'txt', scatter_dimension=0, tiled=...]
    dot_general x33 -> x20, matrix products: 223 us -> 54.5 us  [the longest x5 16.3 us: tn(): lax.dot_general(a, b, (((0,), (0,)), ((), ())), preferred_element_type=F32)]
    unnamed x12 -> x1, waiting for transfers between devices: 148 us -> 0.02 us
    ppermute x0 -> x25, waiting for transfers between devices: none -> 131 us  [the longest x12 95.9 us: halve(): return lax.ppermute(value, BOTH, pairs)]
    pallas_call x0 -> x3, Pallas kernels: none -> 80.9 us  [the longest x1 47.9 us: mlp(): pl.pallas_call(partial(mlp_kernel, pieces), grid_spec=pltpu.PrefetchScala...]
    unnamed x2 -> x1, blocking collectives: 47.2 us -> 7.42 us
    all_gather x1 -> x0, waiting for transfers between devices: 34.6 us -> none  [per_device(): self_kv = lax.all_gather(joined_qkv[..., D:], 'txt', axis=1, tiled=True)]
    convert_element_type x7 -> x8, other arithmetic: 51 us -> 17.1 us  [the longest x1 6.78 us: per_device(): mid_keep, mid_send = plan.split(middle.astype(BF))]
  transfers between devices with their start and end apart: 10 -> 26, of which waited for: 8 -> 13; matrix products, arithmetic and copies ran while one was open for 11% -> 38% of each run, Pallas kernels for 0% -> 7%
where the time goes in v1:
time: 487 us; the launch traced here: 479 us
  waiting for transfers between devices  131 us (27%)
  Pallas kernels  80.9 us (17%)
  other arithmetic  76 us (16%)
  local copies, waits for them, and re-layouts  68.2 us (14%)
  matrix products  59.4 us (12%)
  starting transfers between devices  25.1 us (5%)
  blocking collectives  21.7 us (4%)
  between operations  16.3 us (3%)
    ppermute x12, waiting for transfers between devices, halve(): return lax.ppermute(value, BOTH, pairs)  95.9 us
    pallas_call x1, Pallas kernels, mlp(): pl.pallas_call(partial(mlp_kernel, pieces), grid_spec=pltpu.PrefetchScala...  47.9 us
    ppermute x4, waiting for transfers between devices, shift_y(): return lax.ppermute(value, BOTH, pairs)  33.8 us
    pallas_call x1, Pallas kernels, attend_back(): pl.pallas_call(attend_back_kernel, grid=(pairs,), in_specs=[spec] * 5 + [...  18.4 us
    unnamed x186, local copies, waits for them, and re-layouts  17.2 us
    ppermute x12, starting transfers between devices, halve(): return lax.ppermute(value, BOTH, pairs)  16.9 us
    dot_general x5, matrix products, tn(): lax.dot_general(a, b, (((0,), (0,)), ((), ())), preferred_element_type=F32)  16.3 us
    dot_general x5, matrix products, nn(): lax.dot_general(a, b, (((1,), (0,)), ((), ())), preferred_element_type=F32)  14.7 us
  transfers between devices with their start and end apart: 26, of which 13 were waited for; matrix products, arithmetic and copies ran while one was open for 38% of the time, Pallas kernels for 7%

profile of v1, /device:TPU:0, one launch (start us, length us, event | category | flops | bytes accessed | tf_op | source)
XLA Modules:
  0.0 479.0 jit_solution(1642334481742882322)
XLA Ops:
  11.8 11.9 %collective-permute-done = bf16[256,1024]{1,0:T(8,128)(2,1)S(1)} collective-permute-done((bf16[256,1024]{1,0:T(8,128)(2,1)S(1)}, bf16[256,1024]{1,0:T(8,128)(2,1)S(1)}, u32[]{:S(2)}, u32[]{:S(2)}) %collective-permute-start) | collective-permute-done | bytes 524320 | tf_op jit(solution)/shard_map/ppermute | solution.py:408
  27.4 14.3 %all-gather = bf16[1,128,1024]{2,1,0:T(8,128)(2,1)S(1)} all-gather(bf16[1,32,1024]{2,1,0:T(8,128)(2,1)S(1)} %copy-done.63), channel_id=2, replica_groups=mesh['img'=8,'txt'=4] {'txt'}, dimensions={1}, use_global_device_ids=true | all-gather | bytes 327680 | tf_op jit(solution)/shard_map/all_gather | solution.py:493
  56.9 4.8 convolution_convert_fusion.2
  62.4 14.5 %self_attention.1 = (bf16[1024,512]{1,0:T(8,128)(2,1)S(1)}, f32[4,2,1024]{2,1,0:T(2,128)S(1)}) custom-call(bf16[1024,512]{1,0:T(8,128)(2,1)S(1)} %get-tuple-element.65.q_ref, bf16[1024,512]{1,0:T(8,128)(2,1)S(1)} %get-tuple-element.64.k_ref, bf16[1024,512]{1,0:T(8,128)(2,1)S(1)} %get-tuple-element.63.v_ref), custom_call_target="tpu_custom_call" | custom-call | flops 2147483648 | bytes 4194304 | tf_op jit(solution)/shard_map/self_attention/pallas_call | solution.py:114
  79.5 7.4 %all-reduce.1 = bf16[128]{0:T(256)(128)(2,1)S(1)} all-reduce(bf16[128]{0:T(256)(128)(2,1)S(1)} %dynamic-update-slice), channel_id=3, replica_groups=mesh['img'=8,'txt'=4] {'txt'}, use_global_device_ids=true, to_apply=%add.1 | all-reduce | flops 128 | bytes 512
  90.1 3.3 fusion.57
  99.6 4.9 %fusion.58 = (f32[16,512]{1,0:T(8,128)S(1)}, f32[16,512,128]{1,2,0:T(8,128)}) fusion(pred[128]{0:T(512)(128)(4,1)S(1)} %broadcast_compare_fusion, bf16[512,16,64]{0,2,1:T(8,128)(2,1)S(1)} %bitcast.188, bf16[128,16,64]{0,2,1:T(8,128)(2,1)} %bitcast.209), kind=kOutput, calls=%fused_computation.213 | convolution fusion | flops 138412160 | bytes 5537920 | tf_op jit(solution)/shard_map/sub | solution.py:523
  114.2 47.9 %mlp_both_ways.1 = (f32[512,1024]{1,0:T(8,128)}, f32[512,1024]{1,0:T(8,128)}, bf16[2,512,1024]{2,1,0:T(8,128)(2,1)}, bf16[8,64,4096]{2,1,0:T(8,128)(2,1)}, bf16[8,64,4096]{2,1,0:T(8,128)(2,1)}) custom-call(s32[1]{0:T(128)} %bitcast.22.core_ref, s32[16]{0:T(128)} %fusion.35.rows_from, s32[16]{0:T(128)} %gather_fusion, ...), custom_call_target="tpu_custom_call" | custom-call | flops 25769803776 | bytes 25165824 | tf_op jit(solution)/shard_map/mlp_both_ways/pallas_call | solution.py:326
  162.5 3.8 fusion.3
  179.8 3.9 convolution_convert_fusion.11
  195.4 3.3 convolution_convert_fusion.6
  208.0 10.1 %pad_maximum_fusion = bf16[16,2,32,5120]{3,2,1,0:T(8,128)(2,1)S(1)} fusion(bf16[16,2,32,2048]{3,2,1,0:T(8,128)(2,1)S(1)} %bitcast.175, bf16[16,2,32,1024]{3,2,1,0:T(8,128)(2,1)S(1)} %bitcast.196, bf16[16,2,32,1024]{3,2,1,0:T(8,128)(2,1)S(1)} %convolution_convert_fusion.5, bf16[16,2,32,1024]{3,2,1,0:T(8,128)(2,1)S(1)} %convolution_convert_fusion.6), kind=kLoop, calls=%fused_computation.4 | loop fusion | flops 41943040 | bytes 20971520 | tf_op jit(solution)/shard_map/concatenate | solution.py:570
  229.4 4.6 convolution_convert_fusion.12
  238.5 18.4 %self_attention_back.1 = (bf16[1024,512]{1,0:T(8,128)(2,1)S(1)}, bf16[1024,512]{1,0:T(8,128)(2,1)S(1)}, bf16[1024,512]{1,0:T(8,128)(2,1)S(1)}) custom-call(bf16[1024,512]{1,0:T(8,128)(2,1)S(1)} %copy-done.7, bf16[1024,512]{1,0:T(8,128)(2,1)S(1)} %copy-done.5, bf16[1024,512]{1,0:T(8,128)(2,1)} %copy-done.3, bf16[1024,512]{1,0:T(8,128)(2,1)} %pad_maximum_fusion.12.g_ref, ...), custom_call_target="tpu_custom_call" | custom-call | flops 5368709120 | bytes 8388608 | tf_op jit(solution)/shard_map/self_attention_back/pallas_call | solution.py:176
  259.5 3.4 fusion.14
  263.2 7.9 %convolution_convert_fusion.1 = bf16[1024,1536]{1,0:T(8,128)(2,1)} fusion(f32[1024]{0:T(1024)S(1)} %copy-done.76, f32[1024]{0:T(1024)S(1)} %copy-done.67, bf16[256,1536]{1,0:T(8,128)(2,1)S(1)} %get-tuple-element.60, bf16[256,1536]{1,0:T(8,128)(2,1)S(1)} %get-tuple-element.61, bf16[256,1536]{1,0:T(8,128)(2,1)S(1)} %get-tuple-element.62, ...), kind=kOutput, calls=%fused_computation.24 | convolution fusion | flops 3244818432 | bytes 8404992 | tf_op jit(solution)/shard_map/dot_general | solution.py:34
  272.5 3.9 fusion.6
  276.4 4.6 gather_fusion.1
  284.4 3.0 add_convert_fusion.7
  287.9 3.7 add_convert_fusion
  297.6 13.5 %collective-permute-done.15 = bf16[8,64,1664]{2,1,0:T(8,128)(2,1)S(1)} collective-permute-done((bf16[8,64,1664]{2,1,0:T(8,128)(2,1)S(1)}, bf16[8,64,1664]{2,1,0:T(8,128)(2,1)S(1)}, u32[]{:S(2)}, u32[]{:S(2)}) %collective-permute-start.15) | collective-permute-done | bytes 1703968 | tf_op jit(solution)/shard_map/ppermute | solution.py:412
  316.4 21.9 %collective-permute-done.10 = bf16[256,1024]{1,0:T(8,128)(2,1)} collective-permute-done((bf16[256,1024]{1,0:T(8,128)(2,1)}, bf16[256,1024]{1,0:T(8,128)(2,1)}, u32[]{:S(2)}, u32[]{:S(2)}) %collective-permute-start.10) | collective-permute-done | bytes 524320 | tf_op jit(solution)/shard_map/ppermute | solution.py:408
  338.3 3.1 fusion.20
  343.0 4.4 collective-permute-done.16
  354.5 7.1 %collective-permute-done.17 = bf16[2,64,1664]{2,1,0:T(8,128)(2,1)S(1)} collective-permute-done((bf16[2,64,1664]{2,1,0:T(8,128)(2,1)S(1)}, bf16[2,64,1664]{2,1,0:T(8,128)(2,1)S(1)}, u32[]{:S(2)}, u32[]{:S(2)}) %collective-permute-start.17) | collective-permute-done | bytes 426016 | tf_op jit(solution)/shard_map/ppermute | solution.py:412
  364.5 6.8 %fusion.1 = bf16[16,32,5120]{2,1,0:T(8,128)(2,1)} fusion(bf16[16,32,5120]{2,1,0:T(8,128)(2,1)} %collective-permute-done.20, bf16[16,2,32,5120]{3,2,1,0:T(8,128)(2,1)S(1)} %bitcast.174, s32[]{:T(128)S(6)} %select_n.189), kind=kLoop, calls=%fused_computation.6 | loop fusion | flops 10485760 | bytes 15728644 | tf_op jit(solution)/shard_map/convert_element_type | solution.py:573
  371.3 5.7 %gather_fusion.2 = bf16[16,32,5120]{2,1,0:T(8,128)(2,1)} fusion(bf16[16,32,5120]{2,1,0:T(8,128)(2,1)} %fusion.1, s32[1024]{0:T(1024)S(1)} %pad_clamp_fusion), kind=kCustom, calls=%fused_computation.2 | custom fusion | bytes 10485824 | tf_op jit(solution)/shard_map/jit(_take)/gather | solution.py:454
  386.0 13.6 %collective-permute-done.14 = bf16[1,64,4096]{2,1,0:T(8,128)(2,1)S(1)} collective-permute-done((bf16[1,64,4096]{2,1,0:T(8,128)(2,1)S(1)}, bf16[1,64,4096]{2,1,0:T(8,128)(2,1)S(1)}, u32[]{:S(2)}, u32[]{:S(2)}) %collective-permute-start.14) | collective-permute-done | bytes 524320 | tf_op jit(solution)/shard_map/ppermute | solution.py:412
  399.8 24.6 %collective-permute-done.21 = bf16[8,32,5120]{2,1,0:T(8,128)(2,1)S(1)} collective-permute-done((bf16[8,32,5120]{2,1,0:T(8,128)(2,1)S(1)}, bf16[8,32,5120]{2,1,0:T(8,128)(2,1)S(1)}, u32[]{:S(2)}, u32[]{:S(2)}) %collective-permute-start.21) | collective-permute-done | bytes 2621472 | tf_op jit(solution)/shard_map/ppermute | solution.py:412
  429.4 13.8 %collective-permute-done.22 = bf16[4,32,5120]{2,1,0:T(8,128)(2,1)S(1)} collective-permute-done((bf16[4,32,5120]{2,1,0:T(8,128)(2,1)S(1)}, bf16[4,32,5120]{2,1,0:T(8,128)(2,1)S(1)}, u32[]{:S(2)}, u32[]{:S(2)}) %collective-permute-start.22) | collective-permute-done | bytes 1310752 | tf_op jit(solution)/shard_map/ppermute | solution.py:412
  450.4 7.2 %collective-permute-done.23 = bf16[2,32,5120]{2,1,0:T(8,128)(2,1)} collective-permute-done((bf16[2,32,5120]{2,1,0:T(8,128)(2,1)}, bf16[2,32,5120]{2,1,0:T(8,128)(2,1)}, u32[]{:S(2)}, u32[]{:S(2)}) %collective-permute-start.23) | collective-permute-done | bytes 655392 | tf_op jit(solution)/shard_map/ppermute | solution.py:412
  461.4 9.0 %collective-permute-done.24 = bf16[1,32,5120]{2,1,0:T(8,128)(2,1)S(1)} collective-permute-done((bf16[1,32,5120]{2,1,0:T(8,128)(2,1)S(1)}, bf16[1,32,5120]{2,1,0:T(8,128)(2,1)S(1)}, u32[]{:S(2)}, u32[]{:S(2)}) %collective-permute-start.24) | collective-permute-done | bytes 327712 | tf_op jit(solution)/shard_map/ppermute | solution.py:412
  (357 shorter events, 152.3 us)
Async XLA Ops:
  7.2 100.2 %copy-start = (bf16[1024,1024]{1,0:T(8,128)(2,1)S(1)}, bf16[1024,1024]{1,0:T(8,128)(2,1)}, u32[]{:S(2)}) copy-start(bf16[1024,1024]{1,0:T(8,128)(2,1)} %param.33) | copy-start | bytes 6291460
  7.2 307.7 %reduce-scatter.2.cloned.1.call-start = ((), (), s32[]{:S(2)}) async-start(), calls=%async_computation.1 | async-start | bytes 327680 | tf_op jit(solution)/shard_map/reduce_scatter | solution.py:562
  8.7 15.0 %collective-permute-start = (bf16[256,1024]{1,0:T(8,128)(2,1)S(1)}, bf16[256,1024]{1,0:T(8,128)(2,1)S(1)}, u32[]{:S(2)}, u32[]{:S(2)}) collective-permute-start(bf16[256,1024]{1,0:T(8,128)(2,1)S(1)} %get-tuple-element.94), channel_id=1, source_target_pairs={{0,2},{1,3},{2,0},{3,1},{4,6},{5,7},{6,4},{7,5},{8,10},{9,11},{10,... | collective-permute-start | bytes 1572872 | tf_op jit(solution)/shard_map/ppermute | solution.py:408
  23.8 28.6 %collective-permute-start.1 = (bf16[512,1024]{1,0:T(8,128)(2,1)S(1)}, bf16[512,1024]{1,0:T(8,128)(2,1)}, u32[]{:S(2)}, u32[]{:S(2)}) collective-permute-start(bf16[512,1024]{1,0:T(8,128)(2,1)S(1)} %bitcast.178), channel_id=1, source_target_pairs={{0,1},{1,0},{2,3},{3,2},{4,5},{5,4},{6,7},{7,6},{8,9},{9,8},{10,11... | collective-permute-start | bytes 3145736 | tf_op jit(solution)/shard_map/ppermute | solution.py:400
  25.0 62.7 %collective-permute-start.4 = (bf16[256,1024]{1,0:T(8,128)(2,1)}, bf16[256,1024]{1,0:T(8,128)(2,1)}, u32[]{:S(2)}, u32[]{:S(2)}) collective-permute-start(bf16[256,1024]{1,0:T(8,128)(2,1)} %get-tuple-element.88), channel_id=1, source_target_pairs={{0,2},{1,3},{2,0},{3,1},{4,6},{5,7},{6,4},{7,5},{8,10},{9,11},{10,... | collective-permute-start | bytes 1572872 | tf_op jit(solution)/shard_map/ppermute | solution.py:408
  56.8 206.4 %copy-start.65 = (f32[1024]{0:T(1024)}, f32[1024]{0:T(1024)S(1)}, u32[]{:S(2)}) copy-start(f32[1024]{0:T(1024)S(1)} %add_rsqrt_fusion) | copy-start | bytes 12292
  78.9 11.2 %collective-permute-start.2 = (bf16[512,512]{1,0:T(8,128)(2,1)}, bf16[512,512]{1,0:T(8,128)(2,1)}, u32[]{:S(2)}, u32[]{:S(2)}) collective-permute-start(bf16[512,512]{1,0:T(8,128)(2,1)} %pad_maximum_fusion.15), channel_id=1, source_target_pairs={{0,1},{1,0},{2,3},{3,2},{4,5},{5,4},{6,7},{7,6},{8,9},{9,8},{10,11... | collective-permute-start | bytes 1572872 | tf_op jit(solution)/shard_map/ppermute | solution.py:400
  90.1 23.2 %collective-permute-start.5 = (bf16[512,1024]{1,0:T(8,128)(2,1)}, bf16[512,1024]{1,0:T(8,128)(2,1)}, u32[]{:S(2)}, u32[]{:S(2)}) collective-permute-start(bf16[512,1024]{1,0:T(8,128)(2,1)} %bitcast.27.own_g_ref), channel_id=1, source_target_pairs={{0,1},{1,0},{2,3},{3,2},{4,5},{5,4},{6,7},{7,6},{8,9},{9,8},{10,11... | collective-permute-start | bytes 3145736 | tf_op jit(solution)/shard_map/ppermute | solution.py:400
  111.0 3.1 collective-permute-start.3
  114.2 48.4 %copy-start.70 = (s32[16]{0:T(128)S(1)}, s32[16]{0:T(128)}, u32[]{:S(2)}) copy-start(s32[16]{0:T(128)} %fusion.35.rows_from) | copy-start | bytes 196
  114.2 48.4 %copy-start.19 = (bf16[2,256,1024]{2,1,0:T(8,128)(2,1)S(1)}, bf16[2,256,1024]{2,1,0:T(8,128)(2,1)}, u32[]{:S(2)}) copy-start(bf16[2,256,1024]{2,1,0:T(8,128)(2,1)} %copy-done.17) | copy-start | bytes 3145732
  162.1 5.7 %collective-permute-start.6 = (bf16[2,512,1024]{2,1,0:T(8,128)(2,1)}, bf16[2,512,1024]{2,1,0:T(8,128)(2,1)}, u32[]{:S(2)}, u32[]{:S(2)}) collective-permute-start(bf16[2,512,1024]{2,1,0:T(8,128)(2,1)} %get-tuple-element.28), channel_id=1, source_target_pairs={{0,1},{1,0},{2,3},{3,2},{4,5},{5,4},{6,7},{7,6},{8,9},{9,8},{10,11... | collective-permute-start | bytes 6291464 | tf_op jit(solution)/shard_map/ppermute | solution.py:400
  166.3 121.1 %collective-permute-start.11 = (bf16[8,64,4096]{2,1,0:T(8,128)(2,1)}, bf16[8,64,4096]{2,1,0:T(8,128)(2,1)}, u32[]{:S(2)}, u32[]{:S(2)}) collective-permute-start(bf16[8,64,4096]{2,1,0:T(8,128)(2,1)} %get-tuple-element.35), channel_id=1, source_target_pairs={{0,4},{1,3},{2,6},{3,1},{4,0},{5,7},{6,2},{7,5},{8,12},{9,11},{10,... | collective-permute-start | bytes 12582920 | tf_op jit(solution)/shard_map/ppermute | solution.py:412
  223.8 140.7 %collective-permute-start.20 = (bf16[16,32,5120]{2,1,0:T(8,128)(2,1)}, bf16[16,32,5120]{2,1,0:T(8,128)(2,1)}, u32[]{:S(2)}, u32[]{:S(2)}) collective-permute-start(bf16[16,32,5120]{2,1,0:T(8,128)(2,1)} %dynamic-slice_bitcast_fusion), channel_id=1, source_target_pairs={{0,1},{1,0},{2,3},{3,2},{4,5},{5,4},{6,7},{7,6},{8,9},{9,8},{10,11... | collective-permute-start | bytes 15728648 | tf_op jit(solution)/shard_map/ppermute | solution.py:400
  227.7 7.8 %collective-permute-start.8 = (bf16[512,512]{1,0:T(8,128)(2,1)}, bf16[512,512]{1,0:T(8,128)(2,1)}, u32[]{:S(2)}, u32[]{:S(2)}) collective-permute-start(bf16[512,512]{1,0:T(8,128)(2,1)} %bitcast.169), channel_id=1, source_target_pairs={{0,1},{1,0},{2,3},{3,2},{4,5},{5,4},{6,7},{7,6},{8,9},{9,8},{10,11... | collective-permute-start | bytes 1572872 | tf_op jit(solution)/shard_map/ppermute | solution.py:400
  235.1 81.3 %collective-permute-start.7 = (bf16[256,1024]{1,0:T(8,128)(2,1)}, bf16[256,1024]{1,0:T(8,128)(2,1)}, u32[]{:S(2)}, u32[]{:S(2)}) collective-permute-start(bf16[256,1024]{1,0:T(8,128)(2,1)} %get-tuple-element.85), channel_id=1, source_target_pairs={{0,2},{1,3},{2,0},{3,1},{4,6},{5,7},{6,4},{7,5},{8,10},{9,11},{10,... | collective-permute-start | bytes 1572872 | tf_op jit(solution)/shard_map/ppermute | solution.py:408
  263.1 8.0 %collective-permute-start.9 = (bf16[512,1024]{1,0:T(8,128)(2,1)S(1)}, bf16[512,1024]{1,0:T(8,128)(2,1)S(1)}, u32[]{:S(2)}, u32[]{:S(2)}) collective-permute-start(bf16[512,1024]{1,0:T(8,128)(2,1)S(1)} %slice.352), channel_id=1, source_target_pairs={{0,1},{1,0},{2,3},{3,2},{4,5},{5,4},{6,7},{7,6},{8,9},{9,8},{10,11... | collective-permute-start | bytes 3145736 | tf_op jit(solution)/shard_map/ppermute | solution.py:400
  282.7 28.4 %collective-permute-start.15 = (bf16[8,64,1664]{2,1,0:T(8,128)(2,1)S(1)}, bf16[8,64,1664]{2,1,0:T(8,128)(2,1)S(1)}, u32[]{:S(2)}, u32[]{:S(2)}) collective-permute-start(bf16[8,64,1664]{2,1,0:T(8,128)(2,1)S(1)} %slice.277), channel_id=1, source_target_pairs={{0,4},{1,3},{2,6},{3,1},{4,0},{5,7},{6,2},{7,5},{8,12},{9,11},{10,... | collective-permute-start | bytes 5111816 | tf_op jit(solution)/shard_map/ppermute | solution.py:412
  294.7 55.9 %collective-permute-start.12 = (bf16[4,64,4096]{2,1,0:T(8,128)(2,1)}, bf16[4,64,4096]{2,1,0:T(8,128)(2,1)}, u32[]{:S(2)}, u32[]{:S(2)}) collective-permute-start(bf16[4,64,4096]{2,1,0:T(8,128)(2,1)} %slice.270), channel_id=1, source_target_pairs={{0,2},{1,5},{2,0},{3,7},{4,6},{5,1},{6,4},{7,3},{8,10},{9,13},{10,... | collective-permute-start | bytes 6291464 | tf_op jit(solution)/shard_map/ppermute | solution.py:412
  296.6 41.7 %collective-permute-start.10 = (bf16[256,1024]{1,0:T(8,128)(2,1)}, bf16[256,1024]{1,0:T(8,128)(2,1)}, u32[]{:S(2)}, u32[]{:S(2)}) collective-permute-start(bf16[256,1024]{1,0:T(8,128)(2,1)} %get-tuple-element.75), channel_id=1, source_target_pairs={{0,2},{1,3},{2,0},{3,1},{4,6},{5,7},{6,4},{7,5},{8,10},{9,11},{10,... | collective-permute-start | bytes 1572872 | tf_op jit(solution)/shard_map/ppermute | solution.py:408
  312.5 34.9 %collective-permute-start.16 = (bf16[4,64,1664]{2,1,0:T(8,128)(2,1)}, bf16[4,64,1664]{2,1,0:T(8,128)(2,1)}, u32[]{:S(2)}, u32[]{:S(2)}) collective-permute-start(bf16[4,64,1664]{2,1,0:T(8,128)(2,1)} %slice.279), channel_id=1, source_target_pairs={{0,2},{1,5},{2,0},{3,7},{4,6},{5,1},{6,4},{7,3},{8,10},{9,13},{10,... | collective-permute-start | bytes 2555912 | tf_op jit(solution)/shard_map/ppermute | solution.py:412
  348.8 12.8 %collective-permute-start.17 = (bf16[2,64,1664]{2,1,0:T(8,128)(2,1)S(1)}, bf16[2,64,1664]{2,1,0:T(8,128)(2,1)S(1)}, u32[]{:S(2)}, u32[]{:S(2)}) collective-permute-start(bf16[2,64,1664]{2,1,0:T(8,128)(2,1)S(1)} %slice.281), channel_id=1, source_target_pairs={{0,8},{1,9},{2,10},{3,11},{4,12},{5,13},{6,14},{7,15},{8,0},{9,1},... | collective-permute-start | bytes 1277960 | tf_op jit(solution)/shard_map/ppermute | solution.py:412
  354.1 28.8 %collective-permute-start.13 = (bf16[2,64,4096]{2,1,0:T(8,128)(2,1)}, bf16[2,64,4096]{2,1,0:T(8,128)(2,1)}, u32[]{:S(2)}, u32[]{:S(2)}) collective-permute-start(bf16[2,64,4096]{2,1,0:T(8,128)(2,1)} %slice.272), channel_id=1, source_target_pairs={{0,8},{1,9},{2,10},{3,11},{4,12},{5,13},{6,14},{7,15},{8,0},{9,1},... | collective-permute-start | bytes 3145736 | tf_op jit(solution)/shard_map/ppermute | solution.py:412
  361.8 24.2 %collective-permute-start.18 = (bf16[1,64,1664]{2,1,0:T(8,128)(2,1)S(1)}, bf16[1,64,1664]{2,1,0:T(8,128)(2,1)S(1)}, u32[]{:S(2)}, u32[]{:S(2)}) collective-permute-start(bf16[1,64,1664]{2,1,0:T(8,128)(2,1)S(1)} %slice.283), channel_id=1, source_target_pairs={{0,16},{1,17},{2,18},{3,19},{4,20},{5,21},{6,22},{7,23},{8,24},{9,... | collective-permute-start | bytes 638984 | tf_op jit(solution)/shard_map/ppermute | solution.py:412
  377.0 47.5 %slice-start.3 = ((s8[5242880]{0:T(1024)(128)(4,1)}), s8[4194304]{0:T(1024)(128)(4,1)S(1)}, s32[]{:S(2)}) async-start(s8[5242880]{0:T(1024)(128)(4,1)} %bitcast.176), calls=%async_computation.5 | async-start | bytes 8388608
  379.1 45.4 %collective-permute-start.21 = (bf16[8,32,5120]{2,1,0:T(8,128)(2,1)S(1)}, bf16[8,32,5120]{2,1,0:T(8,128)(2,1)S(1)}, u32[]{:S(2)}, u32[]{:S(2)}) collective-permute-start(bf16[8,32,5120]{2,1,0:T(8,128)(2,1)S(1)} %slice.290), channel_id=1, source_target_pairs={{0,4},{1,3},{2,6},{3,1},{4,0},{5,7},{6,2},{7,5},{8,12},{9,11},{10,... | collective-permute-start | bytes 7864328 | tf_op jit(solution)/shard_map/ppermute | solution.py:412
  384.4 15.2 %collective-permute-start.14 = (bf16[1,64,4096]{2,1,0:T(8,128)(2,1)S(1)}, bf16[1,64,4096]{2,1,0:T(8,128)(2,1)S(1)}, u32[]{:S(2)}, u32[]{:S(2)}) collective-permute-start(bf16[1,64,4096]{2,1,0:T(8,128)(2,1)S(1)} %slice.274), channel_id=1, source_target_pairs={{0,16},{1,17},{2,18},{3,19},{4,20},{5,21},{6,22},{7,23},{8,24},{9,... | collective-permute-start | bytes 1572872 | tf_op jit(solution)/shard_map/ppermute | solution.py:412
  399.8 46.2 %copy-start.43 = (f32[1,32,3712]{2,1,0:T(8,128)}, f32[1,32,3712]{2,1,0:T(8,128)S(1)}, u32[]{:S(2)}) copy-start(f32[1,32,3712]{2,1,0:T(8,128)S(1)} %fusion.29) | copy-start | bytes 1425412
  425.5 17.7 %collective-permute-start.22 = (bf16[4,32,5120]{2,1,0:T(8,128)(2,1)S(1)}, bf16[4,32,5120]{2,1,0:T(8,128)(2,1)S(1)}, u32[]{:S(2)}, u32[]{:S(2)}) collective-permute-start(bf16[4,32,5120]{2,1,0:T(8,128)(2,1)S(1)} %slice.292), channel_id=1, source_target_pairs={{0,2},{1,5},{2,0},{3,7},{4,6},{5,1},{6,4},{7,3},{8,10},{9,13},{10,... | collective-permute-start | bytes 3932168 | tf_op jit(solution)/shard_map/ppermute | solution.py:412
  427.0 1.6 collective-permute-start.19
  444.5 13.2 %collective-permute-start.23 = (bf16[2,32,5120]{2,1,0:T(8,128)(2,1)}, bf16[2,32,5120]{2,1,0:T(8,128)(2,1)}, u32[]{:S(2)}, u32[]{:S(2)}) collective-permute-start(bf16[2,32,5120]{2,1,0:T(8,128)(2,1)} %slice.294), channel_id=1, source_target_pairs={{0,8},{1,9},{2,10},{3,11},{4,12},{5,13},{6,14},{7,15},{8,0},{9,1},... | collective-permute-start | bytes 1966088 | tf_op jit(solution)/shard_map/ppermute | solution.py:412
  459.1 11.3 %collective-permute-start.24 = (bf16[1,32,5120]{2,1,0:T(8,128)(2,1)S(1)}, bf16[1,32,5120]{2,1,0:T(8,128)(2,1)S(1)}, u32[]{:S(2)}, u32[]{:S(2)}) collective-permute-start(bf16[1,32,5120]{2,1,0:T(8,128)(2,1)S(1)} %slice.296), channel_id=1, source_target_pairs={{0,16},{1,17},{2,18},{3,19},{4,20},{5,21},{6,22},{7,23},{8,24},{9,... | collective-permute-start | bytes 983048 | tf_op jit(solution)/shard_map/ppermute | solution.py:412
  (82 other events, 484.4 us)
Sparse Core Ops, SparseCore 0:
  234.1 20.0 reduce-scatter.1
